TPU v7x, 32 devices: a whole 2x2x4 slice. The times are simulated.
32 devices in a mesh: groups: 2 (over x), mult: 16 (over z, y, core).
Axes of the slice: x: 2, y: 2, z: 4, core: 2. Of those that a mesh axis runs over, the one named last changes fastest.
Arguments:
- wavefunction: bfloat16 [4096, 256], P(('groups', 'mult')), parts along dimension 0, may hold values from -6 to 6
- multiplet_spins: int32 [2048], P(('groups', 'mult')), parts along dimension 0, may hold values from 0 to 6
- left_tiles: bfloat16 [7168, 128, 128], P(('groups', 'mult')), parts along dimension 0, may hold values from -0.046875 to 0.046875
- task_info: int32 [7168, 2], P(('groups', 'mult')), parts along dimension 0, may hold values from -4 to 37, as said below
- task_count: int32 [32], P(('groups', 'mult')), parts along dimension 0, may hold values from 28 to 224, as said below
- right_ops: bfloat16 [76, 256, 256], P('groups'), parts along dimension 0, may hold values from -0.375 to 0.375
Outputs:
- applied: float32 [4096, 256], P(('groups', 'mult')), parts along dimension 0
There are 2 independent parts, one for each index of `groups`. A program takes and returns all parts, laid end to end along the dimension named above; each array names one. Nothing has to cross between parts.
Inputs may be any that keep to these rules, and one draw needn't show every extreme that they name: `task_info`: column 0 is the offset from a task's output block to its input block; the input block lies within 4 blocks and inside 0 to 15. Column 1 is the MPO bond index, below 38. `task_count`: at least one block has all 224 slots live.
All inputs are finite; a program needn't handle non-finite values.
Results may differ from a plain program's by a relative error of at most 0.005.
Values may be sent and summed in bfloat16 or wider, within the bound.
A program may use at most 64 MiB of HBM per device.

v0:
```python
import jax
import jax.numpy as jnp
from jax import lax
from jax.sharding import PartitionSpec as P

BAND = 4


def from_behind(block, axis, distance):
    devices = range(lax.axis_size(axis))
    route = [(i - distance, i) for i in devices if i - distance in devices]
    return lax.ppermute(block, axis, route)


def row_roots(multiplet_spins):
    dimensions = (2 * multiplet_spins + 1).astype(jnp.float32)
    return jnp.repeat(jnp.sqrt(dimensions), 2)


def band_source(source, band_width):
    pieces = []
    for offset in range(-band_width, band_width + 1):
        if offset == 0:
            pieces.append(source)
        else:
            pieces.append(from_behind(source, "mult", -offset))
    return jnp.concatenate(pieces, axis=0)


def pick_blocks(blocks_ext, offsets, band_width):
    block_total = blocks_ext.shape[0]
    one_hot = (
        offsets[:, None] + band_width == jnp.arange(block_total, dtype=jnp.int32)[None, :]
    ).astype(jnp.bfloat16)
    picked = jnp.einsum("tb,bjc->tjc", one_hot, blocks_ext, preferred_element_type=jnp.float32)
    return picked.astype(jnp.bfloat16)


def bond_terms(tiles, info, living, blocks_ext, bond_total, band_width):
    picked = pick_blocks(blocks_ext, info[:, 0], band_width)
    product = jnp.einsum("tij,tjc->tic", tiles, picked, preferred_element_type=jnp.float32).astype(
        jnp.bfloat16
    )
    selector = (
        (info[:, 1][:, None] == jnp.arange(bond_total, dtype=jnp.int32)[None, :]) & living[:, None]
    ).astype(jnp.bfloat16)
    return jnp.einsum("ta,tic->iac", selector, product, preferred_element_type=jnp.float32)


def finish_bonds(summed, right_ops):
    block_rows = summed.shape[0]
    bond_total = right_ops.shape[0]
    columns = right_ops.shape[2]
    high_part = summed.astype(jnp.bfloat16)
    low_part = (summed - high_part.astype(jnp.float32)).astype(jnp.bfloat16)
    stacked = jnp.concatenate([high_part, low_part], axis=0).reshape(
        2 * block_rows, bond_total * columns
    )
    result = jnp.dot(
        stacked,
        right_ops.reshape(bond_total * columns, columns),
        preferred_element_type=jnp.float32,
    )
    return result[:block_rows] + result[block_rows:]


def task_sum(left_tiles, task_info, extended, right_ops, live_count, band_width):
    slot_total = left_tiles.shape[0]
    block_rows = left_tiles.shape[1]
    columns = extended.shape[1]
    bond_total = right_ops.shape[0]
    blocks_ext = extended.reshape(2 * band_width + 1, block_rows, columns)
    group_size = min(16, slot_total)
    last_group = (live_count + group_size - 1) // group_size

    def add_group(group_index, running):
        group_first = group_index * group_size
        group_tiles = lax.dynamic_slice_in_dim(left_tiles, group_first, group_size, 0)
        group_info = lax.dynamic_slice_in_dim(task_info, group_first, group_size, 0)
        slot_ids = group_first + jnp.arange(group_size, dtype=jnp.int32)
        living = slot_ids < live_count
        return running + bond_terms(
            group_tiles, group_info, living, blocks_ext, bond_total, band_width
        )

    empty = jnp.zeros((block_rows, bond_total, columns), jnp.float32)
    summed = lax.fori_loop(0, last_group, add_group, empty)
    return finish_bonds(summed, right_ops)


def body(wavefunction, multiplet_spins, left_tiles, task_info, task_count, right_ops):
    roots = row_roots(multiplet_spins)
    source = (wavefunction.astype(jnp.float32) * roots[:, None]).astype(jnp.bfloat16)
    extended = band_source(source, BAND)
    total = task_sum(left_tiles, task_info, extended, right_ops, task_count[0], BAND)
    return total / roots[:, None]


def solution(mesh):
    placed = (
        P(("groups", "mult"), None),
        P(("groups", "mult")),
        P(("groups", "mult"), None, None),
        P(("groups", "mult"), None),
        P(("groups", "mult")),
        P("groups", None, None),
    )
    return jax.shard_map(
        body, mesh=mesh, in_specs=placed, out_specs=P(("groups", "mult"), None), check_vma=False
    )
```

profile of v0, /device:TPU:18, one launch (start us, length us, event | category | flops | bytes accessed | tf_op | source)
XLA Modules:
  0.0 169.4 jit_solution(10411642866873083881)
XLA Ops:
  0.0 0.7 convert_sqrt_fusion
  0.9 0.9 multiply_convert_fusion
  1.8 3.5 %collective-permute-start = (bf16[128,256]{1,0:T(8,128)(2,1)S(1)}, bf16[128,256]{1,0:T(8,128)(2,1)S(1)}, u32[]{:S(2)}, u32[]{:S(2)}) collective-permute-start(bf16[128,256]{1,0:T(8,128)(2,1)S(1)} %multiply_convert_fusion), channel_id=1, source_target_pairs={{0,4},{1,5},{2,6},{3,7},{4,8},{5,9},{6,10},{7,11},{8,12},{9,13},{1... | collective-permute-start | bytes 196616 | tf_op jit(solution)/shard_map/ppermute | solution.py:12
  5.3 2.4 %collective-permute-start.7 = (bf16[128,256]{1,0:T(8,128)(2,1)S(1)}, bf16[128,256]{1,0:T(8,128)(2,1)S(1)}, u32[]{:S(2)}, u32[]{:S(2)}) collective-permute-start(bf16[128,256]{1,0:T(8,128)(2,1)S(1)} %multiply_convert_fusion), channel_id=1, source_target_pairs={{4,0},{5,1},{6,2},{7,3},{8,4},{9,5},{10,6},{11,7},{12,8},{13,9},{1... | collective-permute-start | bytes 196616 | tf_op jit(solution)/shard_map/ppermute | solution.py:12
  7.7 1.9 %collective-permute-start.6 = (bf16[128,256]{1,0:T(8,128)(2,1)S(1)}, bf16[128,256]{1,0:T(8,128)(2,1)S(1)}, u32[]{:S(2)}, u32[]{:S(2)}) collective-permute-start(bf16[128,256]{1,0:T(8,128)(2,1)S(1)} %multiply_convert_fusion), channel_id=1, source_target_pairs={{3,0},{4,1},{5,2},{6,3},{7,4},{8,5},{9,6},{10,7},{11,8},{12,9},{13... | collective-permute-start | bytes 196616 | tf_op jit(solution)/shard_map/ppermute | solution.py:12
  9.6 3.3 %collective-permute-start.5 = (bf16[128,256]{1,0:T(8,128)(2,1)S(1)}, bf16[128,256]{1,0:T(8,128)(2,1)S(1)}, u32[]{:S(2)}, u32[]{:S(2)}) collective-permute-start(bf16[128,256]{1,0:T(8,128)(2,1)S(1)} %multiply_convert_fusion), channel_id=1, source_target_pairs={{2,0},{3,1},{4,2},{5,3},{6,4},{7,5},{8,6},{9,7},{10,8},{11,9},{12,... | collective-permute-start | bytes 196616 | tf_op jit(solution)/shard_map/ppermute | solution.py:12
  12.9 2.2 %collective-permute-start.4 = (bf16[128,256]{1,0:T(8,128)(2,1)S(1)}, bf16[128,256]{1,0:T(8,128)(2,1)S(1)}, u32[]{:S(2)}, u32[]{:S(2)}) collective-permute-start(bf16[128,256]{1,0:T(8,128)(2,1)S(1)} %multiply_convert_fusion), channel_id=1, source_target_pairs={{1,0},{2,1},{3,2},{4,3},{5,4},{6,5},{7,6},{8,7},{9,8},{10,9},{11,1... | collective-permute-start | bytes 196616 | tf_op jit(solution)/shard_map/ppermute | solution.py:12
  15.8 3.1 %collective-permute-start.1 = (bf16[128,256]{1,0:T(8,128)(2,1)S(1)}, bf16[128,256]{1,0:T(8,128)(2,1)S(1)}, u32[]{:S(2)}, u32[]{:S(2)}) collective-permute-start(bf16[128,256]{1,0:T(8,128)(2,1)S(1)} %multiply_convert_fusion), channel_id=1, source_target_pairs={{0,3},{1,4},{2,5},{3,6},{4,7},{5,8},{6,9},{7,10},{8,11},{9,12},{10... | collective-permute-start | bytes 196616 | tf_op jit(solution)/shard_map/ppermute | solution.py:12
  18.9 2.5 %collective-permute-done.1 = bf16[128,256]{1,0:T(8,128)(2,1)S(1)} collective-permute-done((bf16[128,256]{1,0:T(8,128)(2,1)S(1)}, bf16[128,256]{1,0:T(8,128)(2,1)S(1)}, u32[]{:S(2)}, u32[]{:S(2)}) %collective-permute-start.1) | collective-permute-done | bytes 65568 | tf_op jit(solution)/shard_map/ppermute | solution.py:12
  21.4 4.1 %collective-permute-start.2 = (bf16[128,256]{1,0:T(8,128)(2,1)S(1)}, bf16[128,256]{1,0:T(8,128)(2,1)S(1)}, u32[]{:S(2)}, u32[]{:S(2)}) collective-permute-start(bf16[128,256]{1,0:T(8,128)(2,1)S(1)} %multiply_convert_fusion), channel_id=1, source_target_pairs={{0,2},{1,3},{2,4},{3,5},{4,6},{5,7},{6,8},{7,9},{8,10},{9,11},{10,... | collective-permute-start | bytes 196616 | tf_op jit(solution)/shard_map/ppermute | solution.py:12
  25.5 3.0 %collective-permute-done.2 = bf16[128,256]{1,0:T(8,128)(2,1)S(1)} collective-permute-done((bf16[128,256]{1,0:T(8,128)(2,1)S(1)}, bf16[128,256]{1,0:T(8,128)(2,1)S(1)}, u32[]{:S(2)}, u32[]{:S(2)}) %collective-permute-start.2) | collective-permute-done | bytes 65568 | tf_op jit(solution)/shard_map/ppermute | solution.py:12
  28.5 2.3 %collective-permute-start.3 = (bf16[128,256]{1,0:T(8,128)(2,1)S(1)}, bf16[128,256]{1,0:T(8,128)(2,1)S(1)}, u32[]{:S(2)}, u32[]{:S(2)}) collective-permute-start(bf16[128,256]{1,0:T(8,128)(2,1)S(1)} %multiply_convert_fusion), channel_id=1, source_target_pairs={{0,1},{1,2},{2,3},{3,4},{4,5},{5,6},{6,7},{7,8},{8,9},{9,10},{10,1... | collective-permute-start | bytes 196616 | tf_op jit(solution)/shard_map/ppermute | solution.py:12
  30.9 4.1 %collective-permute-done.3 = bf16[128,256]{1,0:T(8,128)(2,1)S(1)} collective-permute-done((bf16[128,256]{1,0:T(8,128)(2,1)S(1)}, bf16[128,256]{1,0:T(8,128)(2,1)S(1)}, u32[]{:S(2)}, u32[]{:S(2)}) %collective-permute-start.3) | collective-permute-done | bytes 65568 | tf_op jit(solution)/shard_map/ppermute | solution.py:12
  35.0 0.9 constant_dynamic-update-slice_fusion.4
  36.0 2.7 %broadcast_in_dim.4 = f32[128,38,256]{2,1,0:T(8,128)} broadcast(f32[]{:T(128)} %constant.29.clone.1), dimensions={} | broadcast | bytes 4980740 | tf_op jit(solution)/shard_map/broadcast_in_dim | solution.py:86
  38.7 122.9 %while.10 = (s32[]{:T(128)}, f32[128,38,256]{2,1,0:T(8,128)}, s32[]{:T(128)}, bf16[224,128,128]{2,1,0:T(8,128)(2,1)}, s32[224,2]{0,1:T(2,128)S(1)}, /*index=5*/b...) while((s32[]{:T(128)}, f32[128,38,256]{2,1,0:T(8,128)}, ...), condition=%wide.region_1.2_spmd, body=%wide.region_0.1_spmd.sunk | while | flops 184747392 | bytes 15270731 | solution.py:87
  38.7 0.7 add_compare_fusion.2
  40.0 1.6 fusion.34
  41.6 5.9 %bitcast_add_fusion.2 = f32[128,38,256]{2,1,0:T(8,128)} fusion(f32[128,38,256]{2,1,0:T(8,128)} %get-tuple-element.120, bf16[16,128,256]{2,1,0:T(8,128)(2,1)S(1)} %fusion.34, s32[16]{0:T(128)S(1)} %get-tuple-element.107, pred[16]{0:T(512)(128)(4,1)S(1)} %add_compare_fusion.2), kind=kOutput, calls=%fused_computation.clone.1 | convolution fusion | flops 41092288 | bytes 11010128 | tf_op jit(solution)/shard_map/while/body/ta,tic->iac/dot_general | solution.py:47
  47.5 0.7 add_compare_fusion.2
  48.2 0.5 fusion.33
  48.7 1.6 fusion.34
  50.3 5.9 %bitcast_add_fusion.2 = f32[128,38,256]{2,1,0:T(8,128)} fusion(f32[128,38,256]{2,1,0:T(8,128)} %get-tuple-element.120, bf16[16,128,256]{2,1,0:T(8,128)(2,1)S(1)} %fusion.34, s32[16]{0:T(128)S(1)} %get-tuple-element.107, pred[16]{0:T(512)(128)(4,1)S(1)} %add_compare_fusion.2), kind=kOutput, calls=%fused_computation.clone.1 | convolution fusion | flops 41092288 | bytes 11010128 | tf_op jit(solution)/shard_map/while/body/ta,tic->iac/dot_general | solution.py:47
  56.2 0.7 add_compare_fusion.2
  57.5 1.6 fusion.34
  59.1 5.9 %bitcast_add_fusion.2 = f32[128,38,256]{2,1,0:T(8,128)} fusion(f32[128,38,256]{2,1,0:T(8,128)} %get-tuple-element.120, bf16[16,128,256]{2,1,0:T(8,128)(2,1)S(1)} %fusion.34, s32[16]{0:T(128)S(1)} %get-tuple-element.107, pred[16]{0:T(512)(128)(4,1)S(1)} %add_compare_fusion.2), kind=kOutput, calls=%fused_computation.clone.1 | convolution fusion | flops 41092288 | bytes 11010128 | tf_op jit(solution)/shard_map/while/body/ta,tic->iac/dot_general | solution.py:47
  65.0 0.7 add_compare_fusion.2
  66.3 1.6 fusion.34
  67.9 5.9 %bitcast_add_fusion.2 = f32[128,38,256]{2,1,0:T(8,128)} fusion(f32[128,38,256]{2,1,0:T(8,128)} %get-tuple-element.120, bf16[16,128,256]{2,1,0:T(8,128)(2,1)S(1)} %fusion.34, s32[16]{0:T(128)S(1)} %get-tuple-element.107, pred[16]{0:T(512)(128)(4,1)S(1)} %add_compare_fusion.2), kind=kOutput, calls=%fused_computation.clone.1 | convolution fusion | flops 41092288 | bytes 11010128 | tf_op jit(solution)/shard_map/while/body/ta,tic->iac/dot_general | solution.py:47
  73.8 0.7 add_compare_fusion.2
  75.1 1.6 fusion.34
  76.7 5.9 %bitcast_add_fusion.2 = f32[128,38,256]{2,1,0:T(8,128)} fusion(f32[128,38,256]{2,1,0:T(8,128)} %get-tuple-element.120, bf16[16,128,256]{2,1,0:T(8,128)(2,1)S(1)} %fusion.34, s32[16]{0:T(128)S(1)} %get-tuple-element.107, pred[16]{0:T(512)(128)(4,1)S(1)} %add_compare_fusion.2), kind=kOutput, calls=%fused_computation.clone.1 | convolution fusion | flops 41092288 | bytes 11010128 | tf_op jit(solution)/shard_map/while/body/ta,tic->iac/dot_general | solution.py:47
  82.6 0.7 add_compare_fusion.2
  83.9 1.6 fusion.34
  85.4 5.9 %bitcast_add_fusion.2 = f32[128,38,256]{2,1,0:T(8,128)} fusion(f32[128,38,256]{2,1,0:T(8,128)} %get-tuple-element.120, bf16[16,128,256]{2,1,0:T(8,128)(2,1)S(1)} %fusion.34, s32[16]{0:T(128)S(1)} %get-tuple-element.107, pred[16]{0:T(512)(128)(4,1)S(1)} %add_compare_fusion.2), kind=kOutput, calls=%fused_computation.clone.1 | convolution fusion | flops 41092288 | bytes 11010128 | tf_op jit(solution)/shard_map/while/body/ta,tic->iac/dot_general | solution.py:47
  91.3 0.7 add_compare_fusion.2
  92.6 1.6 fusion.34
  94.2 5.9 %bitcast_add_fusion.2 = f32[128,38,256]{2,1,0:T(8,128)} fusion(f32[128,38,256]{2,1,0:T(8,128)} %get-tuple-element.120, bf16[16,128,256]{2,1,0:T(8,128)(2,1)S(1)} %fusion.34, s32[16]{0:T(128)S(1)} %get-tuple-element.107, pred[16]{0:T(512)(128)(4,1)S(1)} %add_compare_fusion.2), kind=kOutput, calls=%fused_computation.clone.1 | convolution fusion | flops 41092288 | bytes 11010128 | tf_op jit(solution)/shard_map/while/body/ta,tic->iac/dot_general | solution.py:47
  100.1 0.7 add_compare_fusion.2
  101.4 1.6 fusion.34
  103.0 5.9 %bitcast_add_fusion.2 = f32[128,38,256]{2,1,0:T(8,128)} fusion(f32[128,38,256]{2,1,0:T(8,128)} %get-tuple-element.120, bf16[16,128,256]{2,1,0:T(8,128)(2,1)S(1)} %fusion.34, s32[16]{0:T(128)S(1)} %get-tuple-element.107, pred[16]{0:T(512)(128)(4,1)S(1)} %add_compare_fusion.2), kind=kOutput, calls=%fused_computation.clone.1 | convolution fusion | flops 41092288 | bytes 11010128 | tf_op jit(solution)/shard_map/while/body/ta,tic->iac/dot_general | solution.py:47
  108.9 0.7 add_compare_fusion.2
  110.2 1.6 fusion.34
  111.8 5.9 %bitcast_add_fusion.2 = f32[128,38,256]{2,1,0:T(8,128)} fusion(f32[128,38,256]{2,1,0:T(8,128)} %get-tuple-element.120, bf16[16,128,256]{2,1,0:T(8,128)(2,1)S(1)} %fusion.34, s32[16]{0:T(128)S(1)} %get-tuple-element.107, pred[16]{0:T(512)(128)(4,1)S(1)} %add_compare_fusion.2), kind=kOutput, calls=%fused_computation.clone.1 | convolution fusion | flops 41092288 | bytes 11010128 | tf_op jit(solution)/shard_map/while/body/ta,tic->iac/dot_general | solution.py:47
  117.7 0.7 add_compare_fusion.2
  119.0 1.6 fusion.34
  120.6 5.9 %bitcast_add_fusion.2 = f32[128,38,256]{2,1,0:T(8,128)} fusion(f32[128,38,256]{2,1,0:T(8,128)} %get-tuple-element.120, bf16[16,128,256]{2,1,0:T(8,128)(2,1)S(1)} %fusion.34, s32[16]{0:T(128)S(1)} %get-tuple-element.107, pred[16]{0:T(512)(128)(4,1)S(1)} %add_compare_fusion.2), kind=kOutput, calls=%fused_computation.clone.1 | convolution fusion | flops 41092288 | bytes 11010128 | tf_op jit(solution)/shard_map/while/body/ta,tic->iac/dot_general | solution.py:47
  126.5 0.7 add_compare_fusion.2
  127.7 1.6 fusion.34
  129.3 5.9 %bitcast_add_fusion.2 = f32[128,38,256]{2,1,0:T(8,128)} fusion(f32[128,38,256]{2,1,0:T(8,128)} %get-tuple-element.120, bf16[16,128,256]{2,1,0:T(8,128)(2,1)S(1)} %fusion.34, s32[16]{0:T(128)S(1)} %get-tuple-element.107, pred[16]{0:T(512)(128)(4,1)S(1)} %add_compare_fusion.2), kind=kOutput, calls=%fused_computation.clone.1 | convolution fusion | flops 41092288 | bytes 11010128 | tf_op jit(solution)/shard_map/while/body/ta,tic->iac/dot_general | solution.py:47
  135.2 0.7 add_compare_fusion.2
  136.5 1.6 fusion.34
  138.1 5.9 %bitcast_add_fusion.2 = f32[128,38,256]{2,1,0:T(8,128)} fusion(f32[128,38,256]{2,1,0:T(8,128)} %get-tuple-element.120, bf16[16,128,256]{2,1,0:T(8,128)(2,1)S(1)} %fusion.34, s32[16]{0:T(128)S(1)} %get-tuple-element.107, pred[16]{0:T(512)(128)(4,1)S(1)} %add_compare_fusion.2), kind=kOutput, calls=%fused_computation.clone.1 | convolution fusion | flops 41092288 | bytes 11010128 | tf_op jit(solution)/shard_map/while/body/ta,tic->iac/dot_general | solution.py:47
  144.0 0.7 add_compare_fusion.2
  145.3 1.6 fusion.34
  146.9 5.9 %bitcast_add_fusion.2 = f32[128,38,256]{2,1,0:T(8,128)} fusion(f32[128,38,256]{2,1,0:T(8,128)} %get-tuple-element.120, bf16[16,128,256]{2,1,0:T(8,128)(2,1)S(1)} %fusion.34, s32[16]{0:T(128)S(1)} %get-tuple-element.107, pred[16]{0:T(512)(128)(4,1)S(1)} %add_compare_fusion.2), kind=kOutput, calls=%fused_computation.clone.1 | convolution fusion | flops 41092288 | bytes 11010128 | tf_op jit(solution)/shard_map/while/body/ta,tic->iac/dot_general | solution.py:47
  152.8 0.7 add_compare_fusion.2
  153.5 0.5 fusion.33
  154.1 1.6 fusion.34
  155.7 5.9 %bitcast_add_fusion.2 = f32[128,38,256]{2,1,0:T(8,128)} fusion(f32[128,38,256]{2,1,0:T(8,128)} %get-tuple-element.120, bf16[16,128,256]{2,1,0:T(8,128)(2,1)S(1)} %fusion.34, s32[16]{0:T(128)S(1)} %get-tuple-element.107, pred[16]{0:T(512)(128)(4,1)S(1)} %add_compare_fusion.2), kind=kOutput, calls=%fused_computation.clone.1 | convolution fusion | flops 41092288 | bytes 11010128 | tf_op jit(solution)/shard_map/while/body/ta,tic->iac/dot_general | solution.py:47
  161.6 4.0 %copy.24 = bf16[128,38,256]{2,0,1:T(8,128)(2,1)S(1)} copy(f32[128,38,256]{2,1,0:T(8,128)} %get-tuple-element.43) | data formatting | bytes 7471104 | tf_op jit(solution)/shard_map/while | solution.py:87
  165.6 1.6 subtract_convert_fusion
  167.2 1.4 fusion.17
  168.7 0.7 fusion.20
  (64 shorter events, 8.0 us)
Async XLA Ops:
  0.0 38.7 %copy-start.1 = (s32[224,2]{0,1:T(2,128)S(1)}, s32[224,2]{0,1:T(2,128)}, u32[]{:S(2)}) copy-start(s32[224,2]{0,1:T(2,128)} %param.11) | copy-start | bytes 5380
  1.8 14.0 %collective-permute-start = (bf16[128,256]{1,0:T(8,128)(2,1)S(1)}, bf16[128,256]{1,0:T(8,128)(2,1)S(1)}, u32[]{:S(2)}, u32[]{:S(2)}) collective-permute-start(bf16[128,256]{1,0:T(8,128)(2,1)S(1)} %multiply_convert_fusion), channel_id=1, source_target_pairs={{0,4},{1,5},{2,6},{3,7},{4,8},{5,9},{6,10},{7,11},{8,12},{9,13},{1... | collective-permute-start | bytes 196616 | tf_op jit(solution)/shard_map/ppermute | solution.py:12
  5.3 30.7 %collective-permute-start.7 = (bf16[128,256]{1,0:T(8,128)(2,1)S(1)}, bf16[128,256]{1,0:T(8,128)(2,1)S(1)}, u32[]{:S(2)}, u32[]{:S(2)}) collective-permute-start(bf16[128,256]{1,0:T(8,128)(2,1)S(1)} %multiply_convert_fusion), channel_id=1, source_target_pairs={{4,0},{5,1},{6,2},{7,3},{8,4},{9,5},{10,6},{11,7},{12,8},{13,9},{1... | collective-permute-start | bytes 196616 | tf_op jit(solution)/shard_map/ppermute | solution.py:12
  7.7 28.3 %collective-permute-start.6 = (bf16[128,256]{1,0:T(8,128)(2,1)S(1)}, bf16[128,256]{1,0:T(8,128)(2,1)S(1)}, u32[]{:S(2)}, u32[]{:S(2)}) collective-permute-start(bf16[128,256]{1,0:T(8,128)(2,1)S(1)} %multiply_convert_fusion), channel_id=1, source_target_pairs={{3,0},{4,1},{5,2},{6,3},{7,4},{8,5},{9,6},{10,7},{11,8},{12,9},{13... | collective-permute-start | bytes 196616 | tf_op jit(solution)/shard_map/ppermute | solution.py:12
  9.6 26.3 %collective-permute-start.5 = (bf16[128,256]{1,0:T(8,128)(2,1)S(1)}, bf16[128,256]{1,0:T(8,128)(2,1)S(1)}, u32[]{:S(2)}, u32[]{:S(2)}) collective-permute-start(bf16[128,256]{1,0:T(8,128)(2,1)S(1)} %multiply_convert_fusion), channel_id=1, source_target_pairs={{2,0},{3,1},{4,2},{5,3},{6,4},{7,5},{8,6},{9,7},{10,8},{11,9},{12,... | collective-permute-start | bytes 196616 | tf_op jit(solution)/shard_map/ppermute | solution.py:12
  12.9 23.0 %collective-permute-start.4 = (bf16[128,256]{1,0:T(8,128)(2,1)S(1)}, bf16[128,256]{1,0:T(8,128)(2,1)S(1)}, u32[]{:S(2)}, u32[]{:S(2)}) collective-permute-start(bf16[128,256]{1,0:T(8,128)(2,1)S(1)} %multiply_convert_fusion), channel_id=1, source_target_pairs={{1,0},{2,1},{3,2},{4,3},{5,4},{6,5},{7,6},{8,7},{9,8},{10,9},{11,1... | collective-permute-start | bytes 196616 | tf_op jit(solution)/shard_map/ppermute | solution.py:12
  15.8 5.6 %collective-permute-start.1 = (bf16[128,256]{1,0:T(8,128)(2,1)S(1)}, bf16[128,256]{1,0:T(8,128)(2,1)S(1)}, u32[]{:S(2)}, u32[]{:S(2)}) collective-permute-start(bf16[128,256]{1,0:T(8,128)(2,1)S(1)} %multiply_convert_fusion), channel_id=1, source_target_pairs={{0,3},{1,4},{2,5},{3,6},{4,7},{5,8},{6,9},{7,10},{8,11},{9,12},{10... | collective-permute-start | bytes 196616 | tf_op jit(solution)/shard_map/ppermute | solution.py:12
  21.4 7.1 %collective-permute-start.2 = (bf16[128,256]{1,0:T(8,128)(2,1)S(1)}, bf16[128,256]{1,0:T(8,128)(2,1)S(1)}, u32[]{:S(2)}, u32[]{:S(2)}) collective-permute-start(bf16[128,256]{1,0:T(8,128)(2,1)S(1)} %multiply_convert_fusion), channel_id=1, source_target_pairs={{0,2},{1,3},{2,4},{3,5},{4,6},{5,7},{6,8},{7,9},{8,10},{9,11},{10,... | collective-permute-start | bytes 196616 | tf_op jit(solution)/shard_map/ppermute | solution.py:12
  28.5 6.5 %collective-permute-start.3 = (bf16[128,256]{1,0:T(8,128)(2,1)S(1)}, bf16[128,256]{1,0:T(8,128)(2,1)S(1)}, u32[]{:S(2)}, u32[]{:S(2)}) collective-permute-start(bf16[128,256]{1,0:T(8,128)(2,1)S(1)} %multiply_convert_fusion), channel_id=1, source_target_pairs={{0,1},{1,2},{2,3},{3,4},{4,5},{5,6},{6,7},{7,8},{8,9},{9,10},{10,1... | collective-permute-start | bytes 196616 | tf_op jit(solution)/shard_map/ppermute | solution.py:12
  161.6 4.0 %copy-start = (f32[128,38,256]{2,1,0:T(8,128)S(1)}, f32[128,38,256]{2,1,0:T(8,128)}, u32[]{:S(2)}) copy-start(f32[128,38,256]{2,1,0:T(8,128)} %get-tuple-element.43) | copy-start | bytes 14942212
  161.6 5.6 %slice-start = ((s8[4980736]{0:T(1024)(128)(4,1)}), s8[4194304]{0:T(1024)(128)(4,1)S(1)}, s32[]{:S(2)}) async-start(s8[4980736]{0:T(1024)(128)(4,1)} %bitcast.27), calls=%async_computation | async-start | bytes 8388608
  165.6 1.6 slice-start.1
where the time goes:
time: 171 us; the launch traced here: 169 us
  matrix products  114 us (67%)
  starting transfers between devices  22.8 us (13%)
  other arithmetic  14 us (8%)
  waiting for transfers between devices  9.58 us (6%)
  local copies, waits for them, and re-layouts  8.1 us (5%)
    dot_general x14, matrix products, bond_terms(): jnp.einsum('ta,tic->iac', selector, product, preferred_element_type=jnp.f...  82.6 us
    ppermute x8, starting transfers between devices, from_behind(): return lax.ppermute(block, axis, route)  22.8 us
    dot_general x14, matrix products, bond_terms(): jnp.einsum('tij,tjc->tic', tiles, picked, preferred_element_type=jnp.floa...  22.2 us
    ppermute x8, waiting for transfers between devices, from_behind(): return lax.ppermute(block, axis, route)  9.58 us
    lt x14, other arithmetic, add_group(): living = slot_ids < live_count  9.1 us
    dot_general x14, matrix products, pick_blocks(): jnp.einsum('tb,bjc->tjc', one_hot, blocks_ext, preferred_element_type=jnp...  7.48 us
    while x1, local copies, waits for them, and re-layouts, task_sum(): summed = lax.fori_loop(0, last_group, add_group, empty)  4 us
  transfers between devices with their start and end apart: 8, of which 3 were waited for; matrix products, arithmetic and copies ran while one was open for 1% of the time, Pallas kernels for 0%

commit v1 on v0

v1 whole, which is shorter than its diff:
```python
import functools

import jax
import jax.numpy as jnp
from jax import lax
from jax.experimental import pallas as pl
from jax.experimental.pallas import tpu as pltpu
from jax.sharding import PartitionSpec as P

BAND = 4
GROUP = 16
DISTANCES = tuple(d for k in range(1, BAND + 1) for d in (k, -k))


def in_range(index, total):
    return jnp.logical_and(index >= 0, index < total)


def row_roots(spins, rows):
    mults = spins.shape[1]
    row = lax.broadcasted_iota(jnp.int32, (rows, mults), 0) >> 1
    col = lax.broadcasted_iota(jnp.int32, (rows, mults), 1)
    dims = jnp.where(row == col, 2 * spins + 1, 0).astype(jnp.float32)
    return jnp.sqrt(jnp.sum(dims, axis=1, keepdims=True))


def kernel(
    mult,
    count_ref,
    info_ref,
    spins_ref,
    wave_ref,
    tiles_hbm,
    right_hbm,
    out_ref,
    ext,
    tiles,
    right,
    stacked,
    send_sem,
    recv_sem,
    tile_sem,
    right_sem,
):
    me = lax.axis_index("mult")
    rows = wave_ref.shape[0]
    slots = tiles.shape[0]
    barrier = pltpu.get_barrier_semaphore()
    for d in DISTANCES:
        @pl.when(in_range(me + d, mult))
        def _():
            pl.semaphore_signal(
                barrier,
                inc=1,
                device_id={"mult": me + d},
                device_id_type=pl.DeviceIdType.MESH,
            )

    right_copy = pltpu.make_async_copy(right_hbm, right, right_sem)
    right_copy.start()
    tile_copies = []
    for g in range(slots // GROUP):
        part = pl.ds(g * GROUP, GROUP)
        copy = pltpu.make_async_copy(tiles_hbm.at[part], tiles.at[part], tile_sem.at[g])
        copy.start()

    roots = row_roots(spins_ref[...], rows)
    ext[BAND] = (wave_ref[...].astype(jnp.float32) * roots).astype(jnp.bfloat16)
    ext[2 * BAND + 1] = jnp.zeros_like(wave_ref)
    out_ref[...] = jnp.zeros_like(out_ref)

    neighbours = sum(in_range(me + d, mult).astype(jnp.int32) for d in DISTANCES)
    pl.semaphore_wait(barrier, neighbours)
    copies = []
    for k, d in enumerate(DISTANCES):
        copy = pltpu.make_async_remote_copy(
            src_ref=ext.at[BAND],
            dst_ref=ext.at[BAND - d],
            send_sem=send_sem.at[k],
            recv_sem=recv_sem.at[k],
            device_id={"mult": me + d},
            device_id_type=pl.DeviceIdType.MESH,
        )
        copies.append(copy)
        pl.when(in_range(me + d, mult))(copy.start)
    for d, copy in zip(DISTANCES, copies):
        pl.when(in_range(me - d, mult))(copy.wait_recv)
    right_copy.wait()
    live = count_ref[0]

    def add_group(g, carry):
        first = g * GROUP
        part = pl.ds(first, GROUP)
        pltpu.make_async_copy(tiles_hbm.at[part], tiles.at[part], tile_sem.at[g]).wait()
        lefts = []
        for j in range(GROUP):
            t = first + j
            block = jnp.where(t < live, info_ref[0, t] + BAND, 2 * BAND + 1)
            bond = info_ref[1, t]
            term = jnp.dot(ext[block], right[bond], preferred_element_type=jnp.float32)
            stacked[pl.ds(j * rows, rows), :] = term.astype(jnp.bfloat16)
            lefts.append(tiles[t])
        out_ref[...] += jnp.dot(
            jnp.concatenate(lefts, axis=1), stacked[...], preferred_element_type=jnp.float32
        )
        return carry

    lax.fori_loop(0, slots // GROUP, add_group, 0)
    out_ref[...] = out_ref[...] / roots
    for d, copy in zip(DISTANCES, copies):
        pl.when(in_range(me + d, mult))(copy.wait_send)


def body(mult, wavefunction, multiplet_spins, left_tiles, task_info, task_count, right_ops):
    rows, columns = wavefunction.shape
    slots = left_tiles.shape[0]
    vmem = pl.BlockSpec(memory_space=pltpu.VMEM)
    smem = pl.BlockSpec(memory_space=pltpu.SMEM)
    hbm = pl.BlockSpec(memory_space=pl.ANY)
    return pl.pallas_call(
        functools.partial(kernel, mult),
        out_shape=jax.ShapeDtypeStruct((rows, columns), jnp.float32),
        in_specs=[smem, smem, vmem, vmem, hbm, hbm],
        out_specs=vmem,
        scratch_shapes=[
            pltpu.VMEM((2 * BAND + 2, rows, columns), jnp.bfloat16),
            pltpu.VMEM(left_tiles.shape, jnp.bfloat16),
            pltpu.VMEM(right_ops.shape, jnp.bfloat16),
            pltpu.VMEM((GROUP * rows, columns), jnp.bfloat16),
            pltpu.SemaphoreType.DMA((len(DISTANCES),)),
            pltpu.SemaphoreType.DMA((len(DISTANCES),)),
            pltpu.SemaphoreType.DMA((slots // GROUP,)),
            pltpu.SemaphoreType.DMA,
        ],
        compiler_params=pltpu.CompilerParams(
            collective_id=0, has_side_effects=True, vmem_limit_bytes=60 * 1024 * 1024
        ),
    )(
        task_count,
        task_info.T,
        multiplet_spins.reshape(1, -1),
        wavefunction,
        left_tiles,
        right_ops,
    )


def solution(mesh):
    placed = (
        P(("groups", "mult"), None),
        P(("groups", "mult")),
        P(("groups", "mult"), None, None),
        P(("groups", "mult"), None),
        P(("groups", "mult")),
        P("groups", None, None),
    )
    return jax.shard_map(
        functools.partial(body, mesh.shape["mult"]),
        mesh=mesh,
        in_specs=placed,
        out_specs=P(("groups", "mult"), None),
        check_vma=False,
    )
```

time: 171 us -> 25.2 us (0.15)
  the two profiles are of different devices: /device:TPU:18 before, /device:TPU:0 now
where the time goes in v1:
time: 25.2 us; the launch traced here: 25 us
  Pallas kernels  22.8 us (90%)
  local copies, waits for them, and re-layouts  1.57 us (6%)
  between operations  0.66 us (3%)
    pallas_call x1, Pallas kernels, body(): pl.pallas_call(functools.partial(kernel, mult), out_shape=jax.ShapeDtypeS...  22.8 us
    unnamed x1, local copies, waits for them, and re-layouts  1.57 us

profile of v1, /device:TPU:0, one launch (start us, length us, event | category | flops | bytes accessed | tf_op | source)
XLA Modules:
  0.0 25.0 jit_solution(17242822487413277959)
XLA Ops:
  0.7 22.8 %shard_map.64 = f32[128,256]{1,0:T(8,128)} custom-call(s32[1]{0:T(128)S(6)} %copy.8.count_ref, s32[2,224]{1,0:T(2,128)} %bitcast.2, s32[1,64]{1,0:T(1,128)} %bitcast.3, bf16[128,256]{1,0:T(8,128)(2,1)} %wave_ref.1, bf16[224,128,128]{2,1,0:T(8,128)(2,1)} %tiles_hbm.1, bf16[38,256,256]{2,1,0:T(8,128)(2,1)} %right_hbm.1), custom_call_target="tpu_custom_call" | custom-call | tf_op jit(solution)/shard_map/pallas_call | solution.py:120
  23.5 1.6 %copy.9 = f32[128,256]{1,0:T(8,128)} copy(f32[128,256]{1,0:T(8,128)} %shard_map.64) | data formatting | bytes 262144

commit v2 on v1

v2 whole, which is shorter than its diff:
```python
import functools

import jax
import jax.numpy as jnp
from jax import lax
from jax.experimental import pallas as pl
from jax.experimental.pallas import tpu as pltpu
from jax.sharding import PartitionSpec as P

BAND = 4
GROUP = 32
UNROLL = 4
ZERO_BLOCK = 2 * BAND + 1
HOPS = tuple(d for k in range(2, BAND + 1, 2) for d in (k, -k))


def in_range(index, total):
    return jnp.logical_and(index >= 0, index < total)


def row_roots(spins, rows):
    mults = spins.shape[1]
    row = lax.broadcasted_iota(jnp.int32, (rows, mults), 0) >> 1
    col = lax.broadcasted_iota(jnp.int32, (rows, mults), 1)
    dims = jnp.where(row == col, 2 * spins + 1, 0).astype(jnp.float32)
    return jnp.sqrt(jnp.sum(dims, axis=1, keepdims=True))


def total(condition, values, axis):
    return jnp.sum(jnp.where(condition, values, 0), axis=axis, keepdims=True)


def bond_plan(info, live, bonds, pairs, width):
    slots = info.shape[1]

    def grid(shape, axis):
        return lax.broadcasted_iota(jnp.int32, shape, axis)

    square = (slots, slots)
    slot_down, slot_along = grid(square, 0), grid(square, 1)
    bond_along = jnp.where(grid((1, slots), 1) < live, info[1:2], bonds)
    bond_down = total(slot_down == slot_along, bond_along, 1)
    block_down = total(slot_down == slot_along, info[0:1] + BAND, 1)
    earlier = (bond_down == bond_along) & (slot_along < slot_down)
    rank = total(earlier, 1, 1)

    small = (bonds, bonds)
    low, high = grid(small, 0), grid(small, 1)
    counts = total(grid((bonds, slots), 0) == bond_along, 1, 1)
    half = (counts + 1) >> 1
    half_along = total(low == high, half, 0)
    start = total(high < low, half_along, 1)
    start_along = total(low == high, start, 0)
    base = total(grid((slots, bonds), 1) == bond_down, start_along, 1)
    position = jnp.where(bond_down < bonds, 2 * base + rank, -1)

    marks = grid((slots, width), 0) + (block_down << 16) + (1 << 24)
    order = total(position == grid((slots, width), 1), marks, 0)
    order = jnp.where(order == 0, ZERO_BLOCK << 16, order & ((1 << 24) - 1))
    opens = total((start == grid((bonds, width), 1)) & (counts > 0), 1, 0)
    carries = jnp.where(opens > 0, 0, 1)
    last = jnp.where(counts > 0, start + half - 1, pairs)
    last = total(grid((bonds, width), 0) == grid((bonds, width), 1), last, 0)
    row = grid((8, width), 0)
    return jnp.where(row == 0, order, jnp.where(row == 1, carries, last))


def kernel(
    mult,
    count_ref,
    info_ref,
    spins_ref,
    wave_ref,
    tiles_hbm,
    right_hbm,
    out_ref,
    ext,
    tiles,
    right,
    sums,
    plan_vmem,
    plan,
    send_sem,
    recv_sem,
    pass_sem,
    got_sem,
    tile_sem,
    right_sem,
    plan_sem,
):
    me = lax.axis_index("mult")
    partner = me + 1 - 2 * lax.rem(me, 2)
    is_even = lax.rem(me, 2) == 0
    rows = wave_ref.shape[0]
    slots = tiles.shape[0]
    bonds = right.shape[0]
    pairs = sums.shape[0] - 1
    mesh_id = pl.DeviceIdType.MESH
    barrier = pltpu.get_barrier_semaphore()
    for d in HOPS:
        @pl.when(in_range(me + d, mult))
        def _():
            pl.semaphore_signal(
                barrier, inc=1, device_id={"mult": me + d}, device_id_type=mesh_id
            )
    pl.semaphore_signal(barrier, inc=1, device_id={"mult": partner}, device_id_type=mesh_id)

    roots = row_roots(spins_ref[...], rows)
    ext[BAND] = (wave_ref[...].astype(jnp.float32) * roots).astype(jnp.bfloat16)

    neighbours = sum(in_range(me + d, mult).astype(jnp.int32) for d in HOPS) + 1
    pl.semaphore_wait(barrier, neighbours)
    hops = []
    for k, d in enumerate(HOPS):
        copy = pltpu.make_async_remote_copy(
            src_ref=ext.at[BAND],
            dst_ref=ext.at[BAND - d],
            send_sem=send_sem.at[k],
            recv_sem=recv_sem.at[k],
            device_id={"mult": me + d},
            device_id_type=mesh_id,
        )
        hops.append(copy)
        pl.when(in_range(me + d, mult))(copy.start)

    def hand_over(k, offset):
        to_odd = pltpu.make_async_remote_copy(
            src_ref=ext.at[BAND + offset],
            dst_ref=ext.at[max(BAND + offset - 1, 0)],
            send_sem=pass_sem.at[k],
            recv_sem=got_sem.at[k],
            device_id={"mult": partner},
            device_id_type=mesh_id,
        )
        to_even = pltpu.make_async_remote_copy(
            src_ref=ext.at[BAND + offset],
            dst_ref=ext.at[min(BAND + offset + 1, 2 * BAND)],
            send_sem=pass_sem.at[k],
            recv_sem=got_sem.at[k],
            device_id={"mult": partner},
            device_id_type=mesh_id,
        )
        return to_odd, to_even

    def sends(offset):
        exists = in_range(me + offset, mult)
        odd_wants = jnp.logical_and(exists, is_even) if offset > -BAND else None
        even_wants = jnp.logical_and(exists, jnp.logical_not(is_even)) if offset < BAND else None
        return odd_wants, even_wants

    def gets(offset):
        exists = in_range(partner + offset, mult)
        from_odd = jnp.logical_and(exists, is_even) if offset < BAND else None
        from_even = jnp.logical_and(exists, jnp.logical_not(is_even)) if offset > -BAND else None
        return from_odd, from_even

    passes = [(0, 0)] + [(k + 1, -d) for k, d in enumerate(HOPS)]
    handed = [hand_over(k, offset) for k, offset in passes]

    def when_either(conditions, actions):
        for condition, action in zip(conditions, actions):
            if condition is not None:
                pl.when(condition)(action)

    when_either(sends(0), [c.start for c in handed[0]])

    right_copy = pltpu.make_async_copy(right_hbm, right, right_sem)
    tile_copies = []
    for g in range(slots // GROUP):
        part = pl.ds(g * GROUP, GROUP)
        copy = pltpu.make_async_copy(tiles_hbm.at[part], tiles.at[part], tile_sem.at[g])
        copy.start()
        tile_copies.append(copy)
    right_copy.start()

    ext[ZERO_BLOCK] = jnp.zeros_like(wave_ref)
    sums[pairs] = jnp.zeros_like(wave_ref)
    plan_vmem[...] = bond_plan(info_ref[...], count_ref[0], bonds, pairs, plan_vmem.shape[1])
    plan_copy = pltpu.make_async_copy(plan_vmem, plan, plan_sem)
    plan_copy.start()

    for (k, offset), both, copy, d in zip(passes[1:], handed[1:], hops, HOPS):
        pl.when(in_range(me - d, mult))(copy.wait_recv)
        when_either(sends(offset), [c.start for c in both])
    plan_copy.wait()
    for copy in tile_copies:
        copy.wait()
    for (k, offset), both in zip(passes, handed):
        when_either(gets(offset), [c.wait_recv for c in both])

    def add_pair(p, run):
        first, second = plan[0, 2 * p], plan[0, 2 * p + 1]
        left = jnp.concatenate([tiles[first & 0xFFFF], tiles[second & 0xFFFF]], axis=1)
        source = jnp.concatenate([ext[first >> 16], ext[second >> 16]], axis=0)
        run = jnp.where(plan[1, p] > 0, run, 0.0) + jnp.dot(
            left, source, preferred_element_type=jnp.float32
        )
        sums[p] = run.astype(jnp.bfloat16)
        return run

    lax.fori_loop(0, pairs, add_pair, jnp.zeros(out_ref.shape, jnp.float32), unroll=UNROLL)
    right_copy.wait()
    lefts = [sums[plan[2, a]] for a in range(bonds)]
    out_ref[...] = (
        jnp.dot(
            jnp.concatenate(lefts, axis=1),
            right[...].reshape(bonds * right.shape[1], right.shape[2]),
            preferred_element_type=jnp.float32,
        )
        / roots
    )
    for d, copy in zip(HOPS, hops):
        pl.when(in_range(me + d, mult))(copy.wait_send)
    for (k, offset), both in zip(passes, handed):
        when_either(sends(offset), [c.wait_send for c in both])


def body(mult, wavefunction, multiplet_spins, left_tiles, task_info, task_count, right_ops):
    rows, columns = wavefunction.shape
    slots = left_tiles.shape[0]
    bonds = right_ops.shape[0]
    pairs = -(-((slots + bonds) // 2) // UNROLL) * UNROLL
    width = -(-max(2 * pairs, bonds) // 128) * 128
    vmem = pl.BlockSpec(memory_space=pltpu.VMEM)
    smem = pl.BlockSpec(memory_space=pltpu.SMEM)
    hbm = pl.BlockSpec(memory_space=pl.ANY)
    return pl.pallas_call(
        functools.partial(kernel, mult),
        out_shape=jax.ShapeDtypeStruct((rows, columns), jnp.float32),
        in_specs=[smem, vmem, vmem, vmem, hbm, hbm],
        out_specs=vmem,
        scratch_shapes=[
            pltpu.VMEM((2 * BAND + 2, rows, columns), jnp.bfloat16),
            pltpu.VMEM(left_tiles.shape, jnp.bfloat16),
            pltpu.VMEM(right_ops.shape, jnp.bfloat16),
            pltpu.VMEM((pairs + 1, rows, columns), jnp.bfloat16),
            pltpu.VMEM((8, width), jnp.int32),
            pltpu.SMEM((8, width), jnp.int32),
            pltpu.SemaphoreType.DMA((len(HOPS),)),
            pltpu.SemaphoreType.DMA((len(HOPS),)),
            pltpu.SemaphoreType.DMA((len(HOPS) + 1,)),
            pltpu.SemaphoreType.DMA((len(HOPS) + 1,)),
            pltpu.SemaphoreType.DMA((slots // GROUP,)),
            pltpu.SemaphoreType.DMA,
            pltpu.SemaphoreType.DMA,
        ],
        compiler_params=pltpu.CompilerParams(
            collective_id=0, has_side_effects=True, vmem_limit_bytes=60 * 1024 * 1024
        ),
    )(
        task_count,
        task_info.T,
        multiplet_spins.reshape(1, -1),
        wavefunction,
        left_tiles,
        right_ops,
    )


def solution(mesh):
    placed = (
        P(("groups", "mult"), None),
        P(("groups", "mult")),
        P(("groups", "mult"), None, None),
        P(("groups", "mult"), None),
        P(("groups", "mult")),
        P("groups", None, None),
    )
    return jax.shard_map(
        functools.partial(body, mesh.shape["mult"]),
        mesh=mesh,
        in_specs=placed,
        out_specs=P(("groups", "mult"), None),
        check_vma=False,
    )
```

time: 25.2 us -> 21.4 us (0.85)
  the two profiles are of different devices: /device:TPU:0 before, /device:TPU:1 now
where the time goes in v2:
time: 21.4 us; the launch traced here: 21.2 us
  Pallas kernels  19 us (89%)
  local copies, waits for them, and re-layouts  1.57 us (7%)
  between operations  0.66 us (3%)
    pallas_call x1, Pallas kernels, body(): pl.pallas_call(functools.partial(kernel, mult), out_shape=jax.ShapeDtypeS...  19 us
    unnamed x1, local copies, waits for them, and re-layouts  1.57 us

profile of v2, /device:TPU:1, one launch (start us, length us, event | category | flops | bytes accessed | tf_op | source)
XLA Modules:
  0.0 21.2 jit_solution(7876145422384690457)
XLA Ops:
  0.7 19.0 %shard_map.64 = f32[128,256]{1,0:T(8,128)} custom-call(s32[1]{0:T(128)S(6)} %copy.8.count_ref, s32[2,224]{1,0:T(2,128)} %bitcast.2, s32[1,64]{1,0:T(1,128)} %bitcast.3, bf16[128,256]{1,0:T(8,128)(2,1)} %wave_ref.1, bf16[224,128,128]{2,1,0:T(8,128)(2,1)} %tiles_hbm.1, bf16[38,256,256]{2,1,0:T(8,128)(2,1)} %right_hbm.1), custom_call_target="tpu_custom_call" | custom-call | tf_op jit(solution)/shard_map/pallas_call | solution.py:227
  19.7 1.6 %copy.9 = f32[128,256]{1,0:T(8,128)} copy(f32[128,256]{1,0:T(8,128)} %shard_map.64) | data formatting | bytes 262144

commit v3 on v2

--- a/solution.py
+++ b/solution.py
@@ -9,7 +9,7 @@
 
 BAND = 4
 GROUP = 32
-UNROLL = 4
+UNROLL = 66
 ZERO_BLOCK = 2 * BAND + 1
 HOPS = tuple(d for k in range(2, BAND + 1, 2) for d in (k, -k))
 
@@ -67,13 +67,17 @@
 
 def kernel(
     mult,
+    count_hbm,
+    info_hbm,
+    spins_hbm,
+    wave_hbm,
+    tiles_hbm,
+    right_hbm,
+    out_ref,
     count_ref,
     info_ref,
     spins_ref,
     wave_ref,
-    tiles_hbm,
-    right_hbm,
-    out_ref,
     ext,
     tiles,
     right,
@@ -87,6 +91,7 @@
     tile_sem,
     right_sem,
     plan_sem,
+    small_sem,
 ):
     me = lax.axis_index("mult")
     partner = me + 1 - 2 * lax.rem(me, 2)
@@ -105,6 +110,18 @@
             )
     pl.semaphore_signal(barrier, inc=1, device_id={"mult": partner}, device_id_type=mesh_id)
 
+    small_copies = [
+        pltpu.make_async_copy(source, target, small_sem.at[i])
+        for i, (source, target) in enumerate(
+            [(spins_hbm, spins_ref), (wave_hbm, wave_ref), (info_hbm, info_ref), (count_hbm, count_ref)]
+        )
+    ]
+    for copy in small_copies:
+        copy.start()
+    ext[ZERO_BLOCK] = jnp.zeros_like(wave_ref)
+    sums[pairs] = jnp.zeros_like(wave_ref)
+    for copy in small_copies:
+        copy.wait()
     roots = row_roots(spins_ref[...], rows)
     ext[BAND] = (wave_ref[...].astype(jnp.float32) * roots).astype(jnp.bfloat16)
 
@@ -172,9 +189,6 @@
         copy.start()
         tile_copies.append(copy)
     right_copy.start()
-
-    ext[ZERO_BLOCK] = jnp.zeros_like(wave_ref)
-    sums[pairs] = jnp.zeros_like(wave_ref)
     plan_vmem[...] = bond_plan(info_ref[...], count_ref[0], bonds, pairs, plan_vmem.shape[1])
     plan_copy = pltpu.make_async_copy(plan_vmem, plan, plan_sem)
     plan_copy.start()
@@ -222,14 +236,17 @@
     pairs = -(-((slots + bonds) // 2) // UNROLL) * UNROLL
     width = -(-max(2 * pairs, bonds) // 128) * 128
     vmem = pl.BlockSpec(memory_space=pltpu.VMEM)
-    smem = pl.BlockSpec(memory_space=pltpu.SMEM)
     hbm = pl.BlockSpec(memory_space=pl.ANY)
     return pl.pallas_call(
         functools.partial(kernel, mult),
         out_shape=jax.ShapeDtypeStruct((rows, columns), jnp.float32),
-        in_specs=[smem, vmem, vmem, vmem, hbm, hbm],
+        in_specs=[hbm] * 6,
         out_specs=vmem,
         scratch_shapes=[
+            pltpu.SMEM((1,), jnp.int32),
+            pltpu.VMEM((2, slots), jnp.int32),
+            pltpu.VMEM((1, rows // 2), jnp.int32),
+            pltpu.VMEM((rows, columns), jnp.bfloat16),
             pltpu.VMEM((2 * BAND + 2, rows, columns), jnp.bfloat16),
             pltpu.VMEM(left_tiles.shape, jnp.bfloat16),
             pltpu.VMEM(right_ops.shape, jnp.bfloat16),
@@ -243,6 +260,7 @@
             pltpu.SemaphoreType.DMA((slots // GROUP,)),
             pltpu.SemaphoreType.DMA,
             pltpu.SemaphoreType.DMA,
+            pltpu.SemaphoreType.DMA((4,)),
         ],
         compiler_params=pltpu.CompilerParams(
             collective_id=0, has_side_effects=True, vmem_limit_bytes=60 * 1024 * 1024

time: 21.4 us -> 15.7 us (0.73)
  Pallas kernels: 19 us -> 13.3 us
    pallas_call x1, Pallas kernels: 19 us -> 13.3 us  [body(): pl.pallas_call(functools.partial(kernel, mult), out_shape=jax.ShapeDtypeS...]
where the time goes in v3:
time: 15.7 us; the launch traced here: 15.5 us
  Pallas kernels  13.3 us (85%)
  local copies, waits for them, and re-layouts  1.57 us (10%)
  between operations  0.66 us (4%)
    pallas_call x1, Pallas kernels, body(): pl.pallas_call(functools.partial(kernel, mult), out_shape=jax.ShapeDtypeS...  13.3 us
    unnamed x1, local copies, waits for them, and re-layouts  1.57 us

profile of v3, /device:TPU:1, one launch (start us, length us, event | category | flops | bytes accessed | tf_op | source)
XLA Modules:
  0.0 15.5 jit_solution(9433698168341594599)
XLA Ops:
  0.7 13.3 %shard_map.64 = f32[128,256]{1,0:T(8,128)} custom-call(s32[1]{0:T(128)S(6)} %copy.8.count_hbm, s32[2,224]{1,0:T(2,128)} %bitcast.2, s32[1,64]{1,0:T(1,128)} %bitcast.3, bf16[128,256]{1,0:T(8,128)(2,1)} %wave_hbm.1, bf16[224,128,128]{2,1,0:T(8,128)(2,1)} %tiles_hbm.1, bf16[38,256,256]{2,1,0:T(8,128)(2,1)} %right_hbm.1), custom_call_target="tpu_custom_call" | custom-call | tf_op jit(solution)/shard_map/pallas_call | solution.py:240
  13.9 1.6 %copy.9 = f32[128,256]{1,0:T(8,128)} copy(f32[128,256]{1,0:T(8,128)} %shard_map.64) | data formatting | bytes 262144

commit v4 on v3

--- a/solution.py
+++ b/solution.py
@@ -11,7 +11,7 @@
 GROUP = 32
 UNROLL = 66
 ZERO_BLOCK = 2 * BAND + 1
-HOPS = tuple(d for k in range(2, BAND + 1, 2) for d in (k, -k))
+HOPS = tuple(d for k in range(BAND, 1, -2) for d in (k, -k))
 
 
 def in_range(index, total):

time: 15.7 us -> 15.1 us (0.962)
  Pallas kernels: 13.3 us -> 12.6 us
    pallas_call x1, Pallas kernels: 13.3 us -> 12.6 us  [body(): pl.pallas_call(functools.partial(kernel, mult), out_shape=jax.ShapeDtypeS...]
where the time goes in v4:
time: 15.1 us; the launch traced here: 14.9 us
  Pallas kernels  12.6 us (83%)
  local copies, waits for them, and re-layouts  1.57 us (10%)
  between operations  0.66 us (4%)
    pallas_call x1, Pallas kernels, body(): pl.pallas_call(functools.partial(kernel, mult), out_shape=jax.ShapeDtypeS...  12.6 us
    unnamed x1, local copies, waits for them, and re-layouts  1.57 us

profile of v4, /device:TPU:1, one launch (start us, length us, event | category | flops | bytes accessed | tf_op | source)
XLA Modules:
  0.0 14.9 jit_solution(98445773202962944)
XLA Ops:
  0.7 12.6 %shard_map.64 = f32[128,256]{1,0:T(8,128)} custom-call(s32[1]{0:T(128)S(6)} %copy.8.count_hbm, s32[2,224]{1,0:T(2,128)} %bitcast.2, s32[1,64]{1,0:T(1,128)} %bitcast.3, bf16[128,256]{1,0:T(8,128)(2,1)} %wave_hbm.1, bf16[224,128,128]{2,1,0:T(8,128)(2,1)} %tiles_hbm.1, bf16[38,256,256]{2,1,0:T(8,128)(2,1)} %right_hbm.1), custom_call_target="tpu_custom_call" | custom-call | tf_op jit(solution)/shard_map/pallas_call | solution.py:240
  13.3 1.6 %copy.9 = f32[128,256]{1,0:T(8,128)} copy(f32[128,256]{1,0:T(8,128)} %shard_map.64) | data formatting | bytes 262144
